TPU v7x, 32 devices: a whole 2x2x4 slice. The times are simulated.
32 devices in a mesh: mb: 4 (over y, x), feat: 8 (over z, core).
Axes of the slice: x: 2, y: 2, z: 4, core: 2. Of those that a mesh axis runs over, the one named last changes fastest.
Arguments:
- features: float32 [1024, 262144], P('feat', 'mb'), may hold values from -6 to 6
- tile_rows: int32 [768], P('mb'), may hold values from 0 to 127
- tile_cols: int32 [768], P('mb'), may hold values from 0 to 511
- tile_masks: int32 [768, 128, 128], P('mb'), may hold values 0 or 1
- weight: bfloat16 [1024, 256], replicated, may hold values from -0.5625 to 0.5625
- upstream: bfloat16 [65536, 256], P(('mb', 'feat')), may hold values from -6 to 6
Outputs:
- activation: bfloat16 [65536, 256], P(('mb', 'feat'))
- weight_grad: float32 [1024, 256], P('feat')
All inputs are finite; a program needn't handle non-finite values. No bound on the sum of `tile_masks` on one device may be relied on, other than what follows from the above.
Results may differ from a plain program's by a relative error of at most 0.0063.
Values may be sent and summed in bfloat16 or wider, within the bound.
A program may use at most 192 MiB of HBM per device.

v0:
```python
import jax
import jax.numpy as jnp
from jax import lax
from jax.sharding import PartitionSpec as P

NT = 16384


def smooth_gate(values):
    return 0.5 * values * (1.0 + lax.erf(values * 0.7071067811865476))


def gate_slope(values):
    return (
        0.5 * (1.0 + lax.erf(values * 0.7071067811865476))
        + values * jnp.exp(-0.5 * values * values) * 0.3989422804014327
    )


def neighbor_mean(sources, row_index, col_index, masks):
    feat_cols = sources.shape[0]
    src_count = sources.shape[1]
    tile_size = masks.shape[1]
    row_tiles = NT // tile_size
    blocks = sources.reshape(feat_cols, src_count // tile_size, tile_size)
    picked = jnp.take(blocks, col_index, axis=1)
    weights = masks.astype(jnp.float32)
    contrib = jnp.einsum("fts,tds->tfd", picked, weights, precision=lax.Precision.HIGHEST)
    onehot = (row_index[None, :] == jnp.arange(row_tiles, dtype=jnp.int32)[:, None]).astype(
        jnp.float32
    )
    summed = jnp.einsum("rt,tfd->frd", onehot, contrib, precision=lax.Precision.HIGHEST).reshape(
        feat_cols, NT
    )
    degree = jnp.dot(onehot, jnp.sum(weights, axis=2), precision=lax.Precision.HIGHEST).reshape(NT)
    return ((sources[:, :NT] + summed) / (degree[None, :] + 1.0)).astype(jnp.bfloat16)


def per_device(features, tile_rows, tile_cols, tile_masks, weight, upstream):
    hidden_t = neighbor_mean(features, tile_rows, tile_cols, tile_masks)
    regrouped = lax.all_to_all(hidden_t, "feat", split_axis=1, concat_axis=0, tiled=True)
    preact = lax.dot_general(
        regrouped, weight, (((0,), (0,)), ((), ())), preferred_element_type=jnp.float32
    )
    slopes = (upstream.astype(jnp.float32) * gate_slope(preact)).astype(jnp.bfloat16)
    local_grad = lax.psum_scatter(
        jnp.dot(regrouped, slopes, preferred_element_type=jnp.float32),
        "feat",
        scatter_dimension=0,
        tiled=True,
    )
    activation = smooth_gate(preact).astype(jnp.bfloat16)
    weight_grad = lax.psum(local_grad, "mb")
    return (activation, weight_grad)


def solution(mesh):
    return jax.shard_map(
        per_device,
        mesh=mesh,
        in_specs=(
            P("feat", "mb"),
            P("mb"),
            P("mb"),
            P("mb", None, None),
            P(),
            P(("mb", "feat"), None),
        ),
        out_specs=(P(("mb", "feat"), None), P("feat", None)),
        check_vma=False,
    )
```

profile of v0, /device:TPU:0, one launch (start us, length us, event | category | flops | bytes accessed | tf_op | source)
XLA Modules:
  0.0 372.2 jit_solution(14717296354494510074)
XLA Ops:
  7.2 0.0 copy-start
  7.2 0.0 reduce-scatter.2.cloned.1.call-start
  7.2 0.7 compare_select_fusion
  8.0 0.7 compare_and_fusion
  8.6 33.4 %copy.11 = f32[128,65536]{0,1:T(8,128)} copy(f32[128,65536]{1,0:T(8,128)} %param.6) | data formatting | bytes 67108864 | tf_op args[0]
  42.0 33.4 %copy.13 = f32[128,512,128]{2,0,1:T(8,128)} copy(f32[128,512,128]{0,2,1:T(8,128)} %bitcast.21) | data formatting | bytes 67108864 | tf_op jit(solution)/shard_map/reshape | solution.py:25
  75.5 7.9 %convert_reduce_fusion = f32[192,128]{1,0:T(8,128)S(1)} fusion(s32[192,128,128]{2,1,0:T(8,128)} %param.9), kind=kLoop, calls=%fused_computation.6 | loop fusion | flops 6266880 | bytes 12681216 | tf_op jit(solution)/shard_map/reduce_sum | solution.py:35
  83.4 17.0 %gather_fusion = f32[192,128,128]{2,1,0:T(8,128)} fusion(f32[128,512,128]{2,0,1:T(8,128)} %copy.13, s32[1024]{0:T(1024)S(1)} %pad_clamp_fusion), kind=kCustom, calls=%fused_computation | custom fusion | bytes 25166592 | tf_op jit(solution)/shard_map/jit(_take)/gather | solution.py:26
  100.4 30.6 %fusion = f32[192,128,128]{2,1,0:T(8,128)S(1)} fusion(f32[192,128,128]{2,1,0:T(8,128)} %gather_fusion, s32[192,128,128]{2,1,0:T(8,128)} %param.9, pred[192]{0:T(512)(128)(4,1)S(1)} %compare_and_fusion), kind=kOutput, calls=%fused_computation.1 | convolution fusion | flops 4838129664 | bytes 37748928 | tf_op jit(solution)/shard_map/fts,tds->tfd/dot_general | solution.py:28
  131.0 0.0 copy-done.1
  131.0 25.3 %fusion.10 = f32[128,128,128]{1,2,0:T(8,128)} fusion(f32[192,128,128]{2,1,0:T(8,128)S(1)} %fusion, s32[192]{0:T(256)S(1)} %copy-done.1), kind=kOutput, calls=%fused_computation.13 | convolution fusion | flops 4831862784 | bytes 20972288 | tf_op jit(solution)/shard_map/rt,tfd->frd/dot_general | solution.py:32
  156.3 9.4 %copy.15 = f32[128,128,128]{0,2,1:T(8,128)} copy(f32[128,128,128]{1,2,0:T(8,128)} %fusion.10) | data formatting | bytes 16777216 | tf_op jit(solution)/shard_map/rt,tfd->frd/transpose | solution.py:32
  165.7 0.4 fusion.19
  166.1 11.3 %fusion.7 = bf16[128,16384]{0,1:T(8,128)(2,1)} fusion(f32[128,65536]{0,1:T(8,128)} %copy.11, f32[128,128,128]{0,2,1:T(8,128)} %copy.15, f32[16384]{0:T(1024)S(1)} %fusion.19), kind=kLoop, calls=%fused_computation.10 | loop fusion | flops 6291456 | bytes 21037056 | tf_op jit(solution)/shard_map/convert_element_type | solution.py:36
  177.4 6.5 %copy.16 = bf16[128,8,2048]{2,0,1:T(8,128)(2,1)} copy(bf16[128,8,2048]{0,2,1:T(8,128)(2,1)} %bitcast.22) | data formatting | bytes 8388608 | tf_op jit(solution)/shard_map/all_to_all | solution.py:41
  183.9 100.4 %all_to_all.19 = bf16[128,8,2048]{2,0,1:T(8,128)(2,1)S(1)} all-to-all(bf16[128,8,2048]{2,0,1:T(8,128)(2,1)} %copy.16), channel_id=1, replica_groups=mesh['mb'=4,'feat'=8] {'feat'}, dimensions={1} | all-to-all | bytes 8388608 | tf_op jit(solution)/shard_map/all_to_all | solution.py:41
  284.2 2.5 multiply_convert_fusion
  286.7 2.4 fusion.20
  289.1 0.0 reduce-scatter.2.cloned.1.call-update
  289.2 0.0 all-reduce.2.cloned.1.call-start
  289.2 31.2 %reduce-scatter.2.cloned.1.call-done = f32[128,256]{1,0:T(8,128)} async-done(((f32[1024,256]{1,0:T(8,128)}), f32[128,256]{1,0:T(8,128)}) %reduce-scatter.2.cloned.1.call-update) | async-done | bytes 131088 | tf_op jit(solution)/shard_map/reduce_scatter | solution.py:46
  320.4 0.0 all-reduce.2.cloned.1.call-update
  320.4 43.4 %all-reduce.2.cloned.1.call-done = f32[128,256]{1,0:T(8,128)} async-done(((f32[128,256]{1,0:T(8,128)}), f32[128,256]{1,0:T(8,128)}) %all-reduce.2.cloned.1.call-update) | async-done | bytes 131088 | tf_op jit(solution)/shard_map/psum | solution.py:53
  363.8 1.6 copy.22
  (5 shorter events, 0.0 us)
Async XLA Ops:
  7.2 277.1 %copy-start = (bf16[1024,256]{1,0:T(8,128)(2,1)S(1)}, bf16[1024,256]{1,0:T(8,128)(2,1)}, u32[]{:S(2)}) copy-start(bf16[1024,256]{1,0:T(8,128)(2,1)} %param.10) | copy-start | bytes 1572868
  7.2 313.2 %reduce-scatter.2.cloned.1.call-start = ((), (), s32[]{:S(2)}) async-start(), calls=%async_computation.2 | async-start | bytes 1179648 | tf_op jit(solution)/shard_map/reduce_scatter | solution.py:46
  100.4 30.6 %copy-start.1 = (s32[192]{0:T(256)S(1)}, s32[192]{0:T(256)}, u32[]{:S(2)}) copy-start(s32[192]{0:T(256)} %param.7) | copy-start | bytes 2308
  284.2 2.5 copy-start.2
  289.2 74.6 %all-reduce.2.cloned.1.call-start = ((), (), s32[]{:S(2)}) async-start(), calls=%async_computation.3 | async-start | bytes 262144 | tf_op jit(solution)/shard_map/psum | solution.py:53
Sparse Core Ops, SparseCore 0:
  289.3 31.0 reduce-scatter.1
  323.3 40.4 all-reduce.1
where the time goes:
time: 373 us; the launch traced here: 372 us
  local copies, waits for them, and re-layouts  101 us (27%)
  blocking collectives  100 us (27%)
  waiting for transfers between devices  74.6 us (20%)
  matrix products  61.2 us (16%)
  other arithmetic  20.6 us (6%)
  between operations  14.1 us (4%)
    all_to_all x1, blocking collectives, per_device(): lax.all_to_all(hidden_t, 'feat', split_axis=1, concat_axis=0, tiled=True)  100 us
    psum x1, waiting for transfers between devices, per_device(): weight_grad = lax.psum(local_grad, 'mb')  43.4 us
    unnamed x8, local copies, waits for them, and re-layouts  35 us
    reshape x1, local copies, waits for them, and re-layouts, neighbor_mean(): blocks = sources.reshape(feat_cols, src_count // tile_size, tile_size)  33.4 us
    reduce_scatter x1, waiting for transfers between devices, per_device(): lax.psum_scatter(jnp.dot(regrouped, slopes, preferred_element_type=jnp.fl...  31.2 us
    dot_general x1, matrix products, neighbor_mean(): jnp.einsum('fts,tds->tfd', picked, weights, precision=lax.Precision.HIGHEST)  30.6 us
    dot_general x1, matrix products, neighbor_mean(): jnp.einsum('rt,tfd->frd', onehot, contrib, precision=lax.Precision.HIGHEST)  25.3 us
    gather x1, local copies, waits for them, and re-layouts, neighbor_mean(): picked = jnp.take(blocks, col_index, axis=1)  17 us
  transfers between devices with their start and end apart: 2, of which 2 were waited for; matrix products, arithmetic and copies ran while one was open for 0% of the time, Pallas kernels for 0%

commit v1 on v0

v1 whole, which is shorter than its diff:
```python
import functools
import math

import jax
import jax.numpy as jnp
from jax import lax
from jax.experimental import pallas as pl
from jax.experimental.pallas import tpu as pltpu
from jax.sharding import PartitionSpec as P

VMEM_LIMIT = 60 * 1024 * 1024
DEG_ROWS = 16


def aggregate_kernel(group, rows_ref, cols_ref, feat_ref, mask_ref, out_ref,
                     acc, own, tiles, masks, outbuf, tile_sem, mask_sem, own_sem, out_sem):
    n_tiles, tile = mask_ref.shape[0], mask_ref.shape[1]
    fl = feat_ref.shape[0]
    n_dst, chunks, _, width = out_ref.shape
    n_groups = n_tiles // group
    per_dst = chunks * width

    def fetch(g, _):
        for j in range(group):
            col = pl.multiple_of(cols_ref[g * group + j] * tile, tile)
            pltpu.make_async_copy(
                feat_ref.at[:, pl.ds(col, tile)], tiles.at[g, j], tile_sem.at[g]
            ).start()
        pltpu.make_async_copy(
            mask_ref.at[pl.ds(g * group, group)], masks.at[g], mask_sem.at[g]
        ).start()
        return 0

    lax.fori_loop(0, n_groups, fetch, 0)

    def fetch_own(d, _):
        at = pl.multiple_of(d * per_dst, per_dst)
        pltpu.make_async_copy(
            feat_ref.at[:, pl.ds(at, per_dst)], own.at[d], own_sem.at[d]
        ).start()
        return 0

    lax.fori_loop(0, n_dst, fetch_own, 0)

    def clear(i, _):
        acc[i] = jnp.zeros(acc.shape[1:], jnp.float32)
        return 0

    lax.fori_loop(0, acc.shape[0], clear, 0)

    ones = jnp.ones((DEG_ROWS, tile), jnp.bfloat16)

    def add_group(g, _):
        pltpu.make_async_copy(mask_ref.at[pl.ds(0, group)], masks.at[g], mask_sem.at[g]).wait()
        pltpu.make_async_copy(tiles.at[g], tiles.at[g], tile_sem.at[g]).wait()
        for j in range(group):
            left = jnp.concatenate([tiles[g, j].astype(jnp.bfloat16), ones], axis=0)
            right = masks[g, j].astype(jnp.float32).astype(jnp.bfloat16)
            part = lax.dot_general(
                left, right, (((1,), (1,)), ((), ())), preferred_element_type=jnp.float32
            )
            row = rows_ref[g * group + j]
            acc[row] += part
        return 0

    lax.fori_loop(0, n_groups, add_group, 0)

    blocks = width // tile

    def finish(p, _):
        d, c = p // chunks, p % chunks

        @pl.when(c == 0)
        def _():
            pltpu.make_async_copy(
                feat_ref.at[:, pl.ds(0, per_dst)], own.at[d], own_sem.at[d]
            ).wait()

        for b in range(blocks):
            r = p * blocks + b
            inv = 1.0 / (acc[r, fl:fl + 1, :] + 1.0)
            at = pl.multiple_of(c * width + b * tile, tile)
            outbuf[d, c, :, b * tile:(b + 1) * tile] = (
                (own[d, :, pl.ds(at, tile)] + acc[r, :fl, :]) * inv
            ).astype(jnp.bfloat16)
        pltpu.make_async_copy(outbuf.at[d, c], out_ref.at[d, c], out_sem).start()
        return 0

    lax.fori_loop(0, n_dst * chunks, finish, 0)
    pltpu.make_async_copy(outbuf, out_ref, out_sem).wait()


def aggregate(features, rows, cols, masks, n_dst, chunks, per_dst):
    fl = features.shape[0]
    n_tiles, tile, _ = masks.shape
    width = per_dst // chunks
    group = math.gcd(n_tiles, 8)
    n_groups = n_tiles // group
    return pl.pallas_call(
        functools.partial(aggregate_kernel, group),
        out_shape=jax.ShapeDtypeStruct((n_dst, chunks, fl, width), jnp.bfloat16),
        in_specs=[
            pl.BlockSpec(memory_space=pltpu.SMEM),
            pl.BlockSpec(memory_space=pltpu.SMEM),
            pl.BlockSpec(memory_space=pl.ANY),
            pl.BlockSpec(memory_space=pl.ANY),
        ],
        out_specs=pl.BlockSpec(memory_space=pl.ANY),
        scratch_shapes=[
            pltpu.VMEM((n_dst * per_dst // tile, fl + DEG_ROWS, tile), jnp.float32),
            pltpu.VMEM((n_dst, fl, per_dst), jnp.float32),
            pltpu.VMEM((n_groups, group, fl, tile), jnp.float32),
            pltpu.VMEM((n_groups, group, tile, tile), jnp.int32),
            pltpu.VMEM((n_dst, chunks, fl, width), jnp.bfloat16),
            pltpu.SemaphoreType.DMA((n_groups,)),
            pltpu.SemaphoreType.DMA((n_groups,)),
            pltpu.SemaphoreType.DMA((n_dst,)),
            pltpu.SemaphoreType.DMA,
        ],
        compiler_params=pltpu.CompilerParams(vmem_limit_bytes=VMEM_LIMIT),
        name="aggregate",
    )(rows, cols, features, masks)


def flip(index, offset):
    bit = 1
    while bit <= offset:
        if offset & bit:
            index = index + bit - 2 * bit * ((index // bit) % 2)
        bit *= 2
    return index


def exchange_kernel(n_feat, hid_ref, w_ref, up_ref, act_ref, grad_ref, held, send_sem, recv_sem, own_sem):
    me = lax.axis_index("feat")
    _, chunks, fl, width = hid_ref.shape
    peers = [flip(me, offset) for offset in range(n_feat - 1, 0, -1)]
    mine = pl.ds(pl.multiple_of(me * fl, fl), fl)

    barrier = pltpu.get_barrier_semaphore()
    for peer in peers:
        pl.semaphore_signal(
            barrier, inc=1, device_id={"feat": peer}, device_id_type=pl.DeviceIdType.MESH
        )
    pl.semaphore_wait(barrier, n_feat - 1)

    def send(c, slot, peer):
        return pltpu.make_async_remote_copy(
            src_ref=hid_ref.at[peer, c],
            dst_ref=held.at[c, mine],
            send_sem=send_sem.at[c, slot],
            recv_sem=recv_sem.at[c, slot],
            device_id={"feat": peer},
            device_id_type=pl.DeviceIdType.MESH,
        )

    def keep(c):
        return pltpu.make_async_copy(hid_ref.at[me, c], held.at[c, mine], own_sem.at[c])

    ahead = min(2, chunks)
    for c in range(ahead):
        for slot, peer in enumerate(peers):
            send(c, slot, peer).start()
    for c in range(chunks):
        keep(c).start()

    grad_ref[...] = jnp.zeros_like(grad_ref)

    def work(c, _):
        @pl.when(c + ahead < chunks)
        def _():
            for slot, peer in enumerate(peers):
                send(c, slot, peer).wait_send()
                send(c + ahead, slot, peer).start()

        @pl.when(c + ahead >= chunks)
        def _():
            for slot, peer in enumerate(peers):
                send(c, slot, peer).wait_send()

        keep(c).wait()
        for slot, peer in enumerate(peers):
            send(c, slot, peer).wait_recv()
        hidden = held[c]
        preact = lax.dot_general(
            hidden, w_ref[...], (((0,), (0,)), ((), ())), preferred_element_type=jnp.float32
        )
        rows = pl.ds(pl.multiple_of(c * width, width), width)
        cdf = 0.5 * (1.0 + lax.erf(preact * 0.7071067811865476))
        act_ref[rows, :] = (preact * cdf).astype(jnp.bfloat16)
        slope = cdf + preact * jnp.exp(-0.5 * preact * preact) * 0.3989422804014327
        slopes = (up_ref[rows, :].astype(jnp.float32) * slope).astype(jnp.bfloat16)
        grad_ref[...] += jnp.dot(hidden, slopes, preferred_element_type=jnp.float32)
        return 0

    lax.fori_loop(0, chunks, work, 0)


def exchange(hidden, weight, upstream, n_feat):
    _, chunks, fl, width = hidden.shape
    full, out = weight.shape
    return pl.pallas_call(
        functools.partial(exchange_kernel, n_feat),
        out_shape=(
            jax.ShapeDtypeStruct(upstream.shape, jnp.bfloat16),
            jax.ShapeDtypeStruct((full, out), jnp.float32),
        ),
        in_specs=[
            pl.BlockSpec(memory_space=pl.ANY),
            pl.BlockSpec(memory_space=pltpu.VMEM),
            pl.BlockSpec(memory_space=pltpu.VMEM),
        ],
        out_specs=(
            pl.BlockSpec(memory_space=pltpu.VMEM),
            pl.BlockSpec(memory_space=pltpu.VMEM),
        ),
        scratch_shapes=[
            pltpu.VMEM((chunks, full, width), jnp.bfloat16),
            pltpu.SemaphoreType.DMA((chunks, n_feat - 1)),
            pltpu.SemaphoreType.DMA((chunks, n_feat - 1)),
            pltpu.SemaphoreType.DMA((chunks,)),
        ],
        compiler_params=pltpu.CompilerParams(
            collective_id=0, has_side_effects=True, vmem_limit_bytes=VMEM_LIMIT
        ),
        name="exchange",
    )(hidden, weight, upstream)


def per_device(n_feat, features, tile_rows, tile_cols, tile_masks, weight, upstream):
    per_dst = upstream.shape[0]
    tile = tile_masks.shape[1]
    chunks = math.gcd(per_dst // tile, 4)
    hidden = aggregate(features, tile_rows, tile_cols, tile_masks, n_feat, chunks, per_dst)
    activation, local_grad = exchange(hidden, weight, upstream, n_feat)
    part = lax.psum_scatter(local_grad, "feat", scatter_dimension=0, tiled=True)
    return activation, lax.psum(part, "mb")


def solution(mesh):
    return jax.shard_map(
        functools.partial(per_device, mesh.shape["feat"]),
        mesh=mesh,
        in_specs=(
            P("feat", "mb"),
            P("mb"),
            P("mb"),
            P("mb", None, None),
            P(),
            P(("mb", "feat"), None),
        ),
        out_specs=(P(("mb", "feat"), None), P("feat", None)),
        check_vma=False,
    )
```

time: 373 us -> 209 us (0.56)
  Pallas kernels: 0 us -> 115 us
  blocking collectives: 100 us -> 0 us
  local copies, waits for them, and re-layouts: 101 us -> 3.83 us
  matrix products: 61.2 us -> 0 us
  other arithmetic: 20.6 us -> 0 us
    pallas_call x0 -> x2, Pallas kernels: none -> 115 us  [the longest x1 101 us: exchange(): pl.pallas_call(functools.partial(exchange_kernel, n_feat), out_shape=(jax...]
    all_to_all x1 -> x0, blocking collectives: 100 us -> none  [per_device(): lax.all_to_all(hidden_t, 'feat', split_axis=1, concat_axis=0, tiled=True)]
    dot_general x5 -> x0, matrix products: 61.2 us -> none  [the longest x1 30.6 us: neighbor_mean(): jnp.einsum('fts,tds->tfd', picked, weights, precision=lax.Precision.HIGHEST)]
    reshape x1 -> x0, local copies, waits for them, and re-layouts: 33.4 us -> none  [neighbor_mean(): blocks = sources.reshape(feat_cols, src_count // tile_size, tile_size)]
    unnamed x8 -> x2, local copies, waits for them, and re-layouts: 35 us -> 3.83 us
    gather x1 -> x0, local copies, waits for them, and re-layouts: 17 us -> none  [neighbor_mean(): picked = jnp.take(blocks, col_index, axis=1)]
    convert_element_type x1 -> x0, other arithmetic: 11.3 us -> none  [neighbor_mean(): ((sources[:, :NT] + summed) / (degree[None, :] + 1.0)).astype(jnp.bfloat16)]
    transpose x1 -> x0, local copies, waits for them, and re-layouts: 9.4 us -> none  [neighbor_mean(): jnp.einsum('rt,tfd->frd', onehot, contrib, precision=lax.Precision.HIGHEST)]
where the time goes in v1:
time: 209 us
  Pallas kernels  115 us (55%)
  waiting for transfers between devices  75.8 us (36%)
  between operations  14.1 us (7%)
  local copies, waits for them, and re-layouts  3.83 us (2%)
    pallas_call x1, Pallas kernels, exchange(): pl.pallas_call(functools.partial(exchange_kernel, n_feat), out_shape=(jax...  101 us
    psum x1, waiting for transfers between devices, per_device(): return (activation, lax.psum(part, 'mb'))  43.4 us
    reduce_scatter x1, waiting for transfers between devices, per_device(): part = lax.psum_scatter(local_grad, 'feat', scatter_dimension=0, tiled=True)  32.4 us
    pallas_call x1, Pallas kernels, aggregate(): pl.pallas_call(functools.partial(aggregate_kernel, group), out_shape=jax....  14.1 us
  transfers between devices with their start and end apart: 2, of which 2 were waited for; matrix products, arithmetic and copies ran while one was open for 0% of the time, Pallas kernels for 0%

profile of v1, /device:TPU:0, one launch (start us, length us, event | category | flops | bytes accessed | tf_op | source)
XLA Modules:
  0.0 208.8 jit_solution(10609718696435508899)
XLA Ops:
  7.2 0.0 reduce-scatter.2.cloned.1.call-start
  7.2 14.1 %aggregate.1.hid_ref = bf16[8,4,128,512]{3,2,1,0:T(8,128)(2,1)} custom-call(s32[192]{0:T(256)} %rows_ref.1, s32[192]{0:T(256)} %cols_ref.1, f32[128,65536]{1,0:T(8,128)} %feat_ref.1, s32[192,128,128]{2,1,0:T(8,128)} %mask_ref.1), custom_call_target="tpu_custom_call" | custom-call | tf_op jit(solution)/shard_map/aggregate/pallas_call | solution.py:99
  21.3 100.9 %exchange.1 = (bf16[2048,256]{1,0:T(8,128)(2,1)}, f32[1024,256]{1,0:T(8,128)}) custom-call(bf16[8,4,128,512]{3,2,1,0:T(8,128)(2,1)} %aggregate.1.hid_ref, bf16[1024,256]{1,0:T(8,128)(2,1)} %w_ref.1, bf16[2048,256]{1,0:T(8,128)(2,1)} %up_ref.1), custom_call_target="tpu_custom_call" | custom-call | tf_op jit(solution)/shard_map/exchange/pallas_call | solution.py:202
  122.3 0.0 reduce-scatter.2.cloned.1.call-update
  122.3 0.0 all-reduce.2.cloned.1.call-start
  122.3 32.4 %reduce-scatter.2.cloned.1.call-done = f32[128,256]{1,0:T(8,128)} async-done(((f32[1024,256]{1,0:T(8,128)}), f32[128,256]{1,0:T(8,128)}) %reduce-scatter.2.cloned.1.call-update) | async-done | bytes 131088 | tf_op jit(solution)/shard_map/reduce_scatter | solution.py:236
  154.8 0.0 all-reduce.2.cloned.1.call-update
  154.8 43.4 %all-reduce.2.cloned.1.call-done = f32[128,256]{1,0:T(8,128)} async-done(((f32[128,256]{1,0:T(8,128)}), f32[128,256]{1,0:T(8,128)}) %all-reduce.2.cloned.1.call-update) | async-done | bytes 131088 | tf_op jit(solution)/shard_map/psum | solution.py:237
  198.2 2.3 %copy.10 = bf16[2048,256]{1,0:T(8,128)(2,1)} copy(bf16[2048,256]{1,0:T(8,128)(2,1)} %get-tuple-element.8) | data formatting | bytes 2097152
  200.4 1.6 copy.11
Async XLA Ops:
  7.2 147.6 %reduce-scatter.2.cloned.1.call-start = ((), (), s32[]{:S(2)}) async-start(), calls=%async_computation.1 | async-start | bytes 1179648 | tf_op jit(solution)/shard_map/reduce_scatter | solution.py:236
  122.3 75.9 %all-reduce.2.cloned.1.call-start = ((), (), s32[]{:S(2)}) async-start(), calls=%async_computation.2 | async-start | bytes 262144 | tf_op jit(solution)/shard_map/psum | solution.py:237
Sparse Core Ops, SparseCore 0:
  122.4 32.3 reduce-scatter.1
  157.7 40.4 all-reduce.1

commit v2 on v1

--- a/solution.py
+++ b/solution.py
@@ -131,18 +131,31 @@
     return index
 
 
-def exchange_kernel(n_feat, hid_ref, w_ref, up_ref, act_ref, grad_ref, held, send_sem, recv_sem, own_sem):
+def exchange_kernel(n_feat, n_mb, hid_ref, w_ref, up_ref, act_ref, grad_ref, held, total,
+                    pair_in, mb_out, mb_in, line_out, line_in, parts,
+                    send_sem, recv_sem, own_sem, pair_sem, mb_sem, line_sem, part_sem):
     me = lax.axis_index("feat")
+    my_mb = lax.axis_index("mb")
     _, chunks, fl, width = hid_ref.shape
+    pairs = n_feat // 2
+    share = fl // n_mb
+    wire = mb_out.dtype
+    my_pair = me // 2
+    my_core = me % 2
+    other_core = 1 - my_core
+    partner = flip(me, 1)
     peers = [flip(me, offset) for offset in range(n_feat - 1, 0, -1)]
+    members = [flip(my_mb, offset) for offset in range(n_mb - 1, 0, -1)]
+    order = [flip(my_pair, offset) for offset in range(pairs - 1, -1, -1)]
     mine = pl.ds(pl.multiple_of(me * fl, fl), fl)
+    mesh = pl.DeviceIdType.MESH
 
     barrier = pltpu.get_barrier_semaphore()
     for peer in peers:
-        pl.semaphore_signal(
-            barrier, inc=1, device_id={"feat": peer}, device_id_type=pl.DeviceIdType.MESH
-        )
-    pl.semaphore_wait(barrier, n_feat - 1)
+        pl.semaphore_signal(barrier, inc=1, device_id={"feat": peer}, device_id_type=mesh)
+    for member in members:
+        pl.semaphore_signal(barrier, inc=1, device_id={"mb": member}, device_id_type=mesh)
+    pl.semaphore_wait(barrier, n_feat - 1 + n_mb - 1)
 
     def send(c, slot, peer):
         return pltpu.make_async_remote_copy(
@@ -151,20 +164,60 @@
             send_sem=send_sem.at[c, slot],
             recv_sem=recv_sem.at[c, slot],
             device_id={"feat": peer},
-            device_id_type=pl.DeviceIdType.MESH,
+            device_id_type=mesh,
         )
 
     def keep(c):
         return pltpu.make_async_copy(hid_ref.at[me, c], held.at[c, mine], own_sem.at[c])
 
-    ahead = min(2, chunks)
+    def to_partner(slot, pair):
+        return pltpu.make_async_remote_copy(
+            src_ref=total.at[pair, other_core],
+            dst_ref=pair_in.at[pair],
+            send_sem=pair_sem.at[0, slot],
+            recv_sem=pair_sem.at[1, slot],
+            device_id={"feat": partner},
+            device_id_type=mesh,
+        )
+
+    def to_member(slot, turn, member, pair):
+        return pltpu.make_async_remote_copy(
+            src_ref=mb_out.at[member, pair],
+            dst_ref=mb_in.at[my_mb, pair],
+            send_sem=mb_sem.at[0, slot, turn],
+            recv_sem=mb_sem.at[1, slot, turn],
+            device_id={"mb": member},
+            device_id_type=mesh,
+        )
+
+    def to_line(slot, pair):
+        return pltpu.make_async_remote_copy(
+            src_ref=line_out.at[pair],
+            dst_ref=line_in.at[my_pair],
+            send_sem=line_sem.at[0, slot],
+            recv_sem=line_sem.at[1, slot],
+            device_id={"feat": pair * 2 + my_core},
+            device_id_type=mesh,
+        )
+
+    def to_copy(turn, member):
+        return pltpu.make_async_remote_copy(
+            src_ref=parts.at[my_mb],
+            dst_ref=parts.at[my_mb],
+            send_sem=part_sem.at[0, turn],
+            recv_sem=part_sem.at[1, turn],
+            device_id={"mb": member},
+            device_id_type=mesh,
+        )
+
+    ahead = min(AHEAD, chunks)
     for c in range(ahead):
         for slot, peer in enumerate(peers):
             send(c, slot, peer).start()
     for c in range(chunks):
         keep(c).start()
 
-    grad_ref[...] = jnp.zeros_like(grad_ref)
+    total[...] = jnp.zeros_like(total)
 
     def work(c, _):
         @pl.when(c + ahead < chunks)
@@ -181,29 +234,77 @@
         keep(c).wait()
         for slot, peer in enumerate(peers):
             send(c, slot, peer).wait_recv()
-        hidden = held[c]
         preact = lax.dot_general(
-            hidden, w_ref[...], (((0,), (0,)), ((), ())), preferred_element_type=jnp.float32
+            held[c], w_ref[...], (((0,), (0,)), ((), ())), preferred_element_type=jnp.float32
         )
         rows = pl.ds(pl.multiple_of(c * width, width), width)
         cdf = 0.5 * (1.0 + lax.erf(preact * 0.7071067811865476))
         act_ref[rows, :] = (preact * cdf).astype(jnp.bfloat16)
         slope = cdf + preact * jnp.exp(-0.5 * preact * preact) * 0.3989422804014327
         slopes = (up_ref[rows, :].astype(jnp.float32) * slope).astype(jnp.bfloat16)
-        grad_ref[...] += jnp.dot(hidden, slopes, preferred_element_type=jnp.float32)
+        for slot, pair in enumerate(order):
+            at = pl.ds(pl.multiple_of(pair * (2 * fl), 2 * fl), 2 * fl)
+            term = jnp.dot(held[c, at, :], slopes, preferred_element_type=jnp.float32)
+            total[pair] += term.reshape(2, fl, term.shape[1])
+
+            @pl.when(c == chunks - 1)
+            def _():
+                to_partner(slot, pair).start()
+
         return 0
 
     lax.fori_loop(0, chunks, work, 0)
 
-
-def exchange(hidden, weight, upstream, n_feat):
+    for slot, pair in enumerate(order):
+        to_partner(slot, pair).wait_recv()
+        pair_in[pair] += total[pair, my_core]
+        for turn, member in enumerate(members):
+            at = pl.ds(pl.multiple_of(member * share, share), share)
+            mb_out[member, pair] = pair_in[pair, at, :].astype(wire)
+            to_member(slot, turn, member, pair).start()
+
+    at = pl.ds(pl.multiple_of(my_mb * share, share), share)
+    for slot, pair in enumerate(order):
+        value = pair_in[pair, at, :]
+        for turn, member in enumerate(members):
+            to_member(slot, turn, member, pair).wait_recv()
+            value = value + mb_in[member, pair].astype(jnp.float32)
+        if slot < pairs - 1:
+            line_out[pair] = value.astype(wire)
+            to_line(slot, pair).start()
+
+    for slot, pair in enumerate(order[:-1]):
+        to_line(slot, pair).wait_recv()
+        value = value + line_in[pair].astype(jnp.float32)
+    parts[my_mb] = value
+    for turn, member in enumerate(members):
+        to_copy(turn, member).start()
+
+    for slot, pair in enumerate(order):
+        to_partner(slot, pair).wait_send()
+        for turn, member in enumerate(members):
+            to_member(slot, turn, member, pair).wait_send()
+    for slot, pair in enumerate(order[:-1]):
+        to_line(slot, pair).wait_send()
+    for turn, member in enumerate(members):
+        to_copy(turn, member).wait()
+    for member in range(n_mb):
+        grad_ref[member * share:(member + 1) * share, :] = parts[member]
+
+
+AHEAD = 2
+
+
+def exchange(hidden, weight, upstream, n_feat, n_mb):
     _, chunks, fl, width = hidden.shape
     full, out = weight.shape
+    pairs, share = n_feat // 2, fl // n_mb
+    wire = jnp.bfloat16 if share % 16 == 0 else jnp.float32
     return pl.pallas_call(
-        functools.partial(exchange_kernel, n_feat),
+        functools.partial(exchange_kernel, n_feat, n_mb),
         out_shape=(
             jax.ShapeDtypeStruct(upstream.shape, jnp.bfloat16),
-            jax.ShapeDtypeStruct((full, out), jnp.float32),
+            jax.ShapeDtypeStruct((fl, out), jnp.float32),
         ),
         in_specs=[
             pl.BlockSpec(memory_space=pl.ANY),
@@ -216,9 +317,20 @@
         ),
         scratch_shapes=[
             pltpu.VMEM((chunks, full, width), jnp.bfloat16),
+            pltpu.VMEM((pairs, 2, fl, out), jnp.float32),
+            pltpu.VMEM((pairs, fl, out), jnp.float32),
+            pltpu.VMEM((n_mb, pairs, share, out), wire),
+            pltpu.VMEM((n_mb, pairs, share, out), wire),
+            pltpu.VMEM((pairs, share, out), wire),
+            pltpu.VMEM((pairs, share, out), wire),
+            pltpu.VMEM((n_mb, share, out), jnp.float32),
             pltpu.SemaphoreType.DMA((chunks, n_feat - 1)),
             pltpu.SemaphoreType.DMA((chunks, n_feat - 1)),
             pltpu.SemaphoreType.DMA((chunks,)),
+            pltpu.SemaphoreType.DMA((2, pairs)),
+            pltpu.SemaphoreType.DMA((2, pairs, n_mb - 1)),
+            pltpu.SemaphoreType.DMA((2, pairs - 1)),
+            pltpu.SemaphoreType.DMA((2, n_mb - 1)),
         ],
         compiler_params=pltpu.CompilerParams(
             collective_id=0, has_side_effects=True, vmem_limit_bytes=VMEM_LIMIT
@@ -227,19 +339,17 @@
     )(hidden, weight, upstream)
 
 
-def per_device(n_feat, features, tile_rows, tile_cols, tile_masks, weight, upstream):
+def per_device(n_feat, n_mb, features, tile_rows, tile_cols, tile_masks, weight, upstream):
     per_dst = upstream.shape[0]
     tile = tile_masks.shape[1]
     chunks = math.gcd(per_dst // tile, 4)
     hidden = aggregate(features, tile_rows, tile_cols, tile_masks, n_feat, chunks, per_dst)
-    activation, local_grad = exchange(hidden, weight, upstream, n_feat)
-    part = lax.psum_scatter(local_grad, "feat", scatter_dimension=0, tiled=True)
-    return activation, lax.psum(part, "mb")
+    return exchange(hidden, weight, upstream, n_feat, n_mb)
 
 
 def solution(mesh):
     return jax.shard_map(
-        functools.partial(per_device, mesh.shape["feat"]),
+        functools.partial(per_device, mesh.shape["feat"], mesh.shape["mb"]),
         mesh=mesh,
         in_specs=(
             P("feat", "mb"),

time: 209 us -> 132 us (0.63)
  waiting for transfers between devices: 75.8 us -> 0 us
  between operations: 14.1 us -> 0.65 us
  Pallas kernels: 115 us -> 128 us
    psum x1 -> x0, waiting for transfers between devices: 43.4 us -> none  [per_device(): return (activation, lax.psum(part, 'mb'))]
    reduce_scatter x1 -> x0, waiting for transfers between devices: 32.4 us -> none  [per_device(): part = lax.psum_scatter(local_grad, 'feat', scatter_dimension=0, tiled=True)]
    pallas_call x1, Pallas kernels: 101 us -> 113 us  [exchange(): pl.pallas_call(functools.partial(exchange_kernel, n_feat, n_mb), out_shap...]
  transfers between devices with their start and end apart: 2 -> 0, of which waited for: 2 -> 0; matrix products, arithmetic and copies ran while one was open for 0% -> 0% of each run, Pallas kernels for 0% -> 0%
where the time goes in v2:
time: 132 us
  Pallas kernels  128 us (97%)
  local copies, waits for them, and re-layouts  3.83 us (3%)
    pallas_call x1, Pallas kernels, exchange(): pl.pallas_call(functools.partial(exchange_kernel, n_feat, n_mb), out_shap...  113 us
    pallas_call x1, Pallas kernels, aggregate(): pl.pallas_call(functools.partial(aggregate_kernel, group), out_shape=jax....  14.1 us
    unnamed x2, local copies, waits for them, and re-layouts  3.83 us

profile of v2, /device:TPU:0, one launch (start us, length us, event | category | flops | bytes accessed | tf_op | source)
XLA Modules:
  0.0 132.0 jit_solution(15700730004853279633)
XLA Ops:
  0.6 14.1 %aggregate.1.hid_ref = bf16[8,4,128,512]{3,2,1,0:T(8,128)(2,1)} custom-call(s32[192]{0:T(256)} %rows_ref.1, s32[192]{0:T(256)} %cols_ref.1, f32[128,65536]{1,0:T(8,128)} %feat_ref.1, s32[192,128,128]{2,1,0:T(8,128)} %mask_ref.1), custom_call_target="tpu_custom_call" | custom-call | tf_op jit(solution)/shard_map/aggregate/pallas_call | solution.py:99
  14.7 113.5 %exchange.1 = (bf16[2048,256]{1,0:T(8,128)(2,1)}, f32[128,256]{1,0:T(8,128)}) custom-call(bf16[8,4,128,512]{3,2,1,0:T(8,128)(2,1)} %aggregate.1.hid_ref, bf16[1024,256]{1,0:T(8,128)(2,1)} %w_ref.1, bf16[2048,256]{1,0:T(8,128)(2,1)} %up_ref.1), custom_call_target="tpu_custom_call" | custom-call | tf_op jit(solution)/shard_map/exchange/pallas_call | solution.py:303
  128.2 2.3 %copy.10 = bf16[2048,256]{1,0:T(8,128)(2,1)} copy(bf16[2048,256]{1,0:T(8,128)(2,1)} %get-tuple-element.4) | data formatting | bytes 2097152
  130.5 1.6 %copy.11 = f32[128,256]{1,0:T(8,128)} copy(f32[128,256]{1,0:T(8,128)} %get-tuple-element.5) | data formatting | bytes 262144

commit v3 on v2

--- a/solution.py
+++ b/solution.py
@@ -133,7 +133,8 @@
 
 def exchange_kernel(n_feat, n_mb, hid_ref, w_ref, up_ref, act_ref, grad_ref, held, total,
                     pair_in, mb_out, mb_in, line_out, line_in, parts,
-                    send_sem, recv_sem, own_sem, pair_sem, mb_sem, line_sem, part_sem):
+                    send_sem, recv_sem, own_sem, pair_sem, mb_sem, line_sem, part_sem,
+                    weight, upstream, load_sem):
     me = lax.axis_index("feat")
     my_mb = lax.axis_index("mb")
     _, chunks, fl, width = hid_ref.shape
@@ -150,6 +151,11 @@
     mine = pl.ds(pl.multiple_of(me * fl, fl), fl)
     mesh = pl.DeviceIdType.MESH
 
+    load_weight = pltpu.make_async_copy(w_ref, weight, load_sem.at[0])
+    load_upstream = pltpu.make_async_copy(up_ref, upstream, load_sem.at[1])
+    load_weight.start()
+    load_upstream.start()
+
     barrier = pltpu.get_barrier_semaphore()
     for peer in peers:
         pl.semaphore_signal(barrier, inc=1, device_id={"feat": peer}, device_id_type=mesh)
@@ -218,6 +224,8 @@
         keep(c).start()
 
     total[...] = jnp.zeros_like(total)
+    load_weight.wait()
+    load_upstream.wait()
 
     def work(c, _):
         @pl.when(c + ahead < chunks)
@@ -235,13 +243,13 @@
         for slot, peer in enumerate(peers):
             send(c, slot, peer).wait_recv()
         preact = lax.dot_general(
-            held[c], w_ref[...], (((0,), (0,)), ((), ())), preferred_element_type=jnp.float32
+            held[c], weight[...], (((0,), (0,)), ((), ())), preferred_element_type=jnp.float32
         )
         rows = pl.ds(pl.multiple_of(c * width, width), width)
         cdf = 0.5 * (1.0 + lax.erf(preact * 0.7071067811865476))
         act_ref[rows, :] = (preact * cdf).astype(jnp.bfloat16)
         slope = cdf + preact * jnp.exp(-0.5 * preact * preact) * 0.3989422804014327
-        slopes = (up_ref[rows, :].astype(jnp.float32) * slope).astype(jnp.bfloat16)
+        slopes = (upstream[rows, :].astype(jnp.float32) * slope).astype(jnp.bfloat16)
         for slot, pair in enumerate(order):
             at = pl.ds(pl.multiple_of(pair * (2 * fl), 2 * fl), 2 * fl)
             term = jnp.dot(held[c, at, :], slopes, preferred_element_type=jnp.float32)
@@ -308,8 +316,8 @@
         ),
         in_specs=[
             pl.BlockSpec(memory_space=pl.ANY),
-            pl.BlockSpec(memory_space=pltpu.VMEM),
-            pl.BlockSpec(memory_space=pltpu.VMEM),
+            pl.BlockSpec(memory_space=pl.ANY),
+            pl.BlockSpec(memory_space=pl.ANY),
         ],
         out_specs=(
             pl.BlockSpec(memory_space=pltpu.VMEM),
@@ -331,6 +339,9 @@
             pltpu.SemaphoreType.DMA((2, pairs, n_mb - 1)),
             pltpu.SemaphoreType.DMA((2, pairs - 1)),
             pltpu.SemaphoreType.DMA((2, n_mb - 1)),
+            pltpu.VMEM(weight.shape, weight.dtype),
+            pltpu.VMEM(upstream.shape, upstream.dtype),
+            pltpu.SemaphoreType.DMA((2,)),
         ],
         compiler_params=pltpu.CompilerParams(
             collective_id=0, has_side_effects=True, vmem_limit_bytes=VMEM_LIMIT
@@ -339,12 +350,52 @@
     )(hidden, weight, upstream)
 
 
+def hand_over_kernel(act_ref, grad_ref, act_out, grad_out, act, grad, sem):
+    loads, stores = [], []
+    step = act.shape[1]
+    for k in range(act.shape[0]):
+        rows = pl.ds(k * step, step)
+        loads.append(pltpu.make_async_copy(act_ref.at[rows], act.at[k], sem.at[0, k]))
+        stores.append(pltpu.make_async_copy(act.at[k], act_out.at[rows], sem.at[1, k]))
+    last = act.shape[0]
+    loads.append(pltpu.make_async_copy(grad_ref, grad, sem.at[0, last]))
+    stores.append(pltpu.make_async_copy(grad, grad_out, sem.at[1, last]))
+    for load in loads:
+        load.start()
+    for load, store in zip(loads, stores):
+        load.wait()
+        store.start()
+    for store in stores:
+        store.wait()
+
+
+def hand_over(activation, grad):
+    anywhere = pl.BlockSpec(memory_space=pl.ANY)
+    rows, cols = activation.shape
+    cuts = 4
+    return pl.pallas_call(
+        hand_over_kernel,
+        out_shape=(
+            jax.ShapeDtypeStruct(activation.shape, activation.dtype),
+            jax.ShapeDtypeStruct(grad.shape, grad.dtype),
+        ),
+        in_specs=[anywhere, anywhere],
+        out_specs=(anywhere, anywhere),
+        scratch_shapes=[
+            pltpu.VMEM((cuts, rows // cuts, cols), activation.dtype),
+            pltpu.VMEM(grad.shape, grad.dtype),
+            pltpu.SemaphoreType.DMA((2, cuts + 1)),
+        ],
+        name="hand_over",
+    )(activation, grad)
+
+
 def per_device(n_feat, n_mb, features, tile_rows, tile_cols, tile_masks, weight, upstream):
     per_dst = upstream.shape[0]
     tile = tile_masks.shape[1]
     chunks = math.gcd(per_dst // tile, 4)
     hidden = aggregate(features, tile_rows, tile_cols, tile_masks, n_feat, chunks, per_dst)
-    return exchange(hidden, weight, upstream, n_feat, n_mb)
+    return hand_over(*exchange(hidden, weight, upstream, n_feat, n_mb))
 
 
 def solution(mesh):

time: 132 us -> 129 us (0.977)
  local copies, waits for them, and re-layouts: 3.83 us -> 0 us
    unnamed x2 -> x0, local copies, waits for them, and re-layouts: 3.83 us -> none
    pallas_call x0 -> x1, Pallas kernels: none -> 2.04 us  [hand_over(): pl.pallas_call(hand_over_kernel, out_shape=(jax.ShapeDtypeStruct(activati...]
where the time goes in v3:
time: 129 us
  Pallas kernels  128 us (99%)
    pallas_call x1, Pallas kernels, exchange(): pl.pallas_call(functools.partial(exchange_kernel, n_feat, n_mb), out_shap...  112 us
    pallas_call x1, Pallas kernels, aggregate(): pl.pallas_call(functools.partial(aggregate_kernel, group), out_shape=jax....  14.1 us

profile of v3, /device:TPU:0, one launch (start us, length us, event | category | flops | bytes accessed | tf_op | source)
XLA Modules:
  0.0 129.0 jit_solution(1300944179979327431)
XLA Ops:
  0.6 14.1 %aggregate.1.hid_ref = bf16[8,4,128,512]{3,2,1,0:T(8,128)(2,1)} custom-call(s32[192]{0:T(256)} %rows_ref.1, s32[192]{0:T(256)} %cols_ref.1, f32[128,65536]{1,0:T(8,128)} %feat_ref.1, s32[192,128,128]{2,1,0:T(8,128)} %mask_ref.1), custom_call_target="tpu_custom_call" | custom-call | tf_op jit(solution)/shard_map/aggregate/pallas_call | solution.py:99
  14.8 112.2 %exchange.1 = (bf16[2048,256]{1,0:T(8,128)(2,1)}, f32[128,256]{1,0:T(8,128)}) custom-call(bf16[8,4,128,512]{3,2,1,0:T(8,128)(2,1)} %aggregate.1.hid_ref, bf16[1024,256]{1,0:T(8,128)(2,1)} %w_ref.1, bf16[2048,256]{1,0:T(8,128)(2,1)} %up_ref.1), custom_call_target="tpu_custom_call" | custom-call | tf_op jit(solution)/shard_map/exchange/pallas_call | solution.py:311
  127.0 2.0 %hand_over.1 = (bf16[2048,256]{1,0:T(8,128)(2,1)}, f32[128,256]{1,0:T(8,128)}) custom-call(bf16[2048,256]{1,0:T(8,128)(2,1)} %get-tuple-element.4.act_ref, f32[128,256]{1,0:T(8,128)} %get-tuple-element.5.grad_ref), custom_call_target="tpu_custom_call" | custom-call | tf_op jit(solution)/shard_map/hand_over/pallas_call | solution.py:376

commit v4 on v3

--- a/solution.py
+++ b/solution.py
@@ -31,7 +31,8 @@
         ).start()
         return 0
 
-    lax.fori_loop(0, n_groups, fetch, 0)
+    early = min(n_groups, 8)
+    lax.fori_loop(0, early, fetch, 0)
 
     def fetch_own(d, _):
         at = pl.multiple_of(d * per_dst, per_dst)
@@ -51,6 +52,10 @@
     ones = jnp.ones((DEG_ROWS, tile), jnp.bfloat16)
 
     def add_group(g, _):
+        @pl.when(g + early < n_groups)
+        def _():
+            fetch(g + early, 0)
+
         pltpu.make_async_copy(mask_ref.at[pl.ds(0, group)], masks.at[g], mask_sem.at[g]).wait()
         pltpu.make_async_copy(tiles.at[g], tiles.at[g], tile_sem.at[g]).wait()
         for j in range(group):

time: 129 us -> 131 us (1.016)
  Pallas kernels: 128 us -> 130 us
    pallas_call x1, Pallas kernels: 14.1 us -> 15.7 us  [aggregate(): pl.pallas_call(functools.partial(aggregate_kernel, group), out_shape=jax....]
where the time goes in v4:
time: 131 us
  Pallas kernels  130 us (99%)
    pallas_call x1, Pallas kernels, exchange(): pl.pallas_call(functools.partial(exchange_kernel, n_feat, n_mb), out_shap...  112 us
    pallas_call x1, Pallas kernels, aggregate(): pl.pallas_call(functools.partial(aggregate_kernel, group), out_shape=jax....  15.7 us

profile of v4, /device:TPU:0, one launch (start us, length us, event | category | flops | bytes accessed | tf_op | source)
XLA Modules:
  0.0 130.6 jit_solution(17343617875412861905)
XLA Ops:
  0.6 15.7 %aggregate.1.hid_ref = bf16[8,4,128,512]{3,2,1,0:T(8,128)(2,1)} custom-call(s32[192]{0:T(256)} %rows_ref.1, s32[192]{0:T(256)} %cols_ref.1, f32[128,65536]{1,0:T(8,128)} %feat_ref.1, s32[192,128,128]{2,1,0:T(8,128)} %mask_ref.1), custom_call_target="tpu_custom_call" | custom-call | tf_op jit(solution)/shard_map/aggregate/pallas_call | solution.py:104
  16.3 112.2 %exchange.1 = (bf16[2048,256]{1,0:T(8,128)(2,1)}, f32[128,256]{1,0:T(8,128)}) custom-call(bf16[8,4,128,512]{3,2,1,0:T(8,128)(2,1)} %aggregate.1.hid_ref, bf16[1024,256]{1,0:T(8,128)(2,1)} %w_ref.1, bf16[2048,256]{1,0:T(8,128)(2,1)} %up_ref.1), custom_call_target="tpu_custom_call" | custom-call | tf_op jit(solution)/shard_map/exchange/pallas_call | solution.py:316
  128.5 2.0 %hand_over.1 = (bf16[2048,256]{1,0:T(8,128)(2,1)}, f32[128,256]{1,0:T(8,128)}) custom-call(bf16[2048,256]{1,0:T(8,128)(2,1)} %get-tuple-element.4.act_ref, f32[128,256]{1,0:T(8,128)} %get-tuple-element.5.grad_ref), custom_call_target="tpu_custom_call" | custom-call | tf_op jit(solution)/shard_map/hand_over/pallas_call | solution.py:381
